TPU v7x, 32 devices: a whole 2x2x4 slice. The times are simulated.
32 devices in a mesh: groups: 2 (over x), tensor: 16 (over z, y, core).
Axes of the slice: x: 2, y: 2, z: 4, core: 2. Of those that a mesh axis runs over, the one named last changes fastest.
Arguments:
- hidden_in: bfloat16 [7, 4096, 1024], P(None, 'tensor', 'groups'), parts along dimension 2, may hold values from -6 to 6
- out_grad: bfloat16 [1024, 8192], P('groups'), parts along dimension 0, may hold values from -6 to 6
- down_weight: bfloat16 [7, 4096, 8192], P(None, 'tensor'), may hold values from -0.03125 to 0.03125
- hidden_signs: int32 [3, 7, 4096], replicated, may hold values 0 or 1
- grad_signs: int32 [3, 8192], replicated, may hold values 0 or 1
- hidden_picks: int32 [64], replicated, may hold values from 0 to 28671
- grad_picks: int32 [64], replicated, may hold values from 0 to 8191
- seq_lengths: int32 [16], P('groups'), parts along dimension 0, may hold values from 16 to 64, as said below
Outputs:
- input_grad: bfloat16 [7, 4096, 1024], P(None, 'tensor', 'groups'), parts along dimension 2
- example_sketch: float32 [16, 4096], P('groups', 'tensor'), parts along dimension 0
There are 2 independent parts, one for each index of `groups`. A program takes and returns all parts, laid end to end along the dimension named above; an argument that names none is the same for every part. Nothing has to cross between parts.
Inputs may be any that keep to these rules, and one draw needn't show every extreme that they name: `hidden_picks`: a flat hidden unit index q * 4096 + r. `seq_lengths`: live tokens stand at the start of each sequence; in every draw some sequence is full and some has 16.
All inputs are finite; a program needn't handle non-finite values.
Results may differ from a plain program's by a relative error of at most 0.001.
Values may be sent and summed in bfloat16 or wider, within the bound.
A program may use at most 192 MiB of HBM per device.

v0:
```python
import math

import jax
import jax.numpy as jnp
from jax import lax
from jax.sharding import PartitionSpec as P

highest = lax.Precision.HIGHEST


def from_partner(array, axis, bit):
    return lax.ppermute(array, axis, [(i, i ^ 1 << bit) for i in range(lax.axis_size(axis))])


def parity_sign(first_ids, second_ids):
    parity_sum = jnp.zeros_like(first_ids + second_ids)
    for position in range(16):
        step_size = 2**position
        parity_sum = parity_sum + first_ids // step_size % 2 * (second_ids // step_size % 2)
    return (1 - 2 * (parity_sum % 2)).astype(jnp.float32)


def walsh_table(length):
    indices = jnp.arange(length, dtype=jnp.int32)
    return parity_sign(indices[:, None], indices[None, :])


def split_length(length):
    bits_count = length.bit_length() - 1
    first_len = 2 ** (bits_count // 2)
    return (first_len, length // first_len)


def walsh_last(values, length):
    first_len, second_len = split_length(length)
    shaped = values.reshape(values.shape[0], first_len, second_len)
    shaped = jnp.einsum("ac,ncb->nab", walsh_table(first_len), shaped, precision=highest)
    shaped = jnp.einsum("bd,nad->nab", walsh_table(second_len), shaped, precision=highest)
    return shaped.reshape(values.shape) / math.sqrt(length)


def make_mask(positions, seq_lengths, seq_len):
    owner_seq = positions // seq_len
    seq_ids = jnp.arange(seq_lengths.shape[0], dtype=jnp.int32)
    inside = (positions % seq_len)[None, :] < seq_lengths[:, None]
    return ((owner_seq[None, :] == seq_ids[:, None]) & inside).astype(jnp.float32)


def body(
    hidden_in,
    out_grad,
    down_weight,
    hidden_signs,
    grad_signs,
    hidden_picks,
    grad_picks,
    seq_lengths,
):
    devices_count = lax.axis_size("tensor")
    device_rank = lax.axis_index("tensor")
    blocks, local_rows, tokens = hidden_in.shape
    block_len = local_rows * devices_count
    width = out_grad.shape[1]
    sketch_dim = hidden_picks.shape[0]
    seq_count = seq_lengths.shape[0]
    seq_len = tokens // seq_count
    flat_weight = down_weight.reshape(blocks * local_rows, width)
    input_grad = lax.dot_general(
        flat_weight, out_grad, (((1,), (1,)), ((), ())), preferred_element_type=jnp.float32
    )
    input_grad = input_grad.astype(jnp.bfloat16).reshape(blocks, local_rows, tokens)
    hidden_sign = (1 - 2 * hidden_signs).astype(jnp.float32)
    local_sign = lax.dynamic_slice_in_dim(hidden_sign, device_rank * local_rows, local_rows, 2)
    local_table = walsh_table(local_rows)
    mixed = hidden_in.astype(jnp.float32) * local_sign[0][:, :, None]
    bit_total = devices_count.bit_length() - 1
    for section_num in range(2):
        mixed = jnp.einsum("ac,qct->qat", local_table, mixed, precision=highest)
        for bit_index in range(bit_total):
            partner = from_partner(mixed, "tensor", bit_index)
            upper = device_rank // 2**bit_index % 2 == 1
            mixed = jnp.where(upper, partner - mixed, mixed + partner)
        mixed = mixed * (local_sign[section_num + 1][:, :, None] / math.sqrt(block_len))
    pick_block = hidden_picks // block_len
    pick_row = hidden_picks % block_len
    own_rows = device_rank * local_rows + jnp.arange(local_rows, dtype=jnp.int32)
    last_table = parity_sign(pick_row[:, None], own_rows[None, :]) / math.sqrt(block_len)
    per_block = jnp.einsum("kl,qlt->qkt", last_table, mixed, precision=highest)
    chooser = (pick_block[None, :] == jnp.arange(blocks, dtype=jnp.int32)[:, None]).astype(
        jnp.float32
    )
    partial_proj = jnp.sum(chooser[:, :, None] * per_block, axis=0)
    hidden_proj = lax.psum(partial_proj, "tensor")
    grad_sign = (1 - 2 * grad_signs).astype(jnp.float32)
    column_ids = jnp.arange(width, dtype=jnp.int32)
    final_table = parity_sign(column_ids[:, None], grad_picks[None, :]) / math.sqrt(width)
    mixed_grad = out_grad.astype(jnp.float32) * grad_sign[0][None, :]
    mixed_grad = walsh_last(mixed_grad, width) * grad_sign[1][None, :]
    mixed_grad = walsh_last(mixed_grad, width) * grad_sign[2][None, :]
    grad_proj = jnp.dot(mixed_grad, final_table, precision=highest)
    positions = jnp.arange(tokens, dtype=jnp.int32)
    live_mask = make_mask(positions, seq_lengths, seq_len)
    weighted = live_mask[:, None, :] * hidden_proj[None, :, :]
    full_sketch = jnp.einsum("skt,tb->skb", weighted, grad_proj, precision=highest).reshape(
        seq_count, sketch_dim * sketch_dim
    )
    column_share = sketch_dim * sketch_dim // devices_count
    example_sketch = lax.dynamic_slice_in_dim(
        full_sketch, device_rank * column_share, column_share, 1
    )
    return (input_grad, example_sketch)


def solution(mesh):
    in_specs = (
        P(None, "tensor", "groups"),
        P("groups", None),
        P(None, "tensor", None),
        P(),
        P(),
        P(),
        P(),
        P("groups"),
    )
    out_specs = (P(None, "tensor", "groups"), P("groups", "tensor"))
    return jax.shard_map(body, mesh=mesh, in_specs=in_specs, out_specs=out_specs, check_vma=False)
```

profile of v0, /device:TPU:8, one launch (start us, length us, event | category | flops | bytes accessed | tf_op | source)
XLA Modules:
  0.0 839.1 jit_solution(1321384139854107768)
XLA Ops:
  7.3 0.7 fusion.207
  8.1 10.0 %fusion.33 = f32[7,256,512]{1,2,0:T(8,128)} fusion(bf16[7,256,512]{2,1,0:T(8,128)(2,1)} %param.8, f32[7,256]{1,0:T(8,128)S(1)} %get-tuple-element.9, s32[256]{0:T(256)S(1)} %get-tuple-element.105, s32[256]{0:T(256)S(1)} %get-tuple-element.106, s32[256]{0:T(256)S(1)} %get-tuple-element.107, s32[256]{0:T(256)S(1)} %get-tuple-element.108, ...), kind=kOutput, calls=%fused_computation.42 | convolution fusion | flops 2823356416 | bytes 5528576 | tf_op jit(solution)/shard_map/ac,qct->qat/dot_general | solution.py:78
  18.1 6.7 collective-permute-done
  24.8 5.4 add_select_fusion.5
  30.2 1.5 collective-permute-start.1
  31.8 80.2 %collective-permute-done.1 = f32[7,256,512]{1,2,0:T(8,128)} collective-permute-done((f32[7,256,512]{1,2,0:T(8,128)}, f32[7,256,512]{1,2,0:T(8,128)}, u32[]{:S(2)}, u32[]{:S(2)}) %collective-permute-start.1) | collective-permute-done | bytes 3670048 | tf_op jit(solution)/shard_map/ppermute | solution.py:12
  111.9 5.4 add_select_fusion.4
  117.7 80.5 %collective-permute-done.2 = f32[7,256,512]{1,2,0:T(8,128)} collective-permute-done((f32[7,256,512]{1,2,0:T(8,128)}, f32[7,256,512]{1,2,0:T(8,128)}, u32[]{:S(2)}, u32[]{:S(2)}) %collective-permute-start.2) | collective-permute-done | bytes 3670048 | tf_op jit(solution)/shard_map/ppermute | solution.py:12
  198.2 5.4 add_select_fusion.3
  203.7 2.6 collective-permute-start.3
  206.4 11.4 %multiply_bitcast_fusion = f32[64,8,64,128]{3,1,2,0:T(8,128)} fusion(bf16[512,8192]{1,0:T(8,128)(2,1)} %param.9, f32[8192]{0:T(1024)S(1)} %bitcast.52), kind=kLoop, calls=%fused_computation.7 | loop fusion | flops 8388608 | bytes 25198592
  217.8 144.4 %collective-permute-done.3 = f32[7,256,512]{1,2,0:T(8,128)} collective-permute-done((f32[7,256,512]{1,2,0:T(8,128)}, f32[7,256,512]{1,2,0:T(8,128)}, u32[]{:S(2)}, u32[]{:S(2)}) %collective-permute-start.3) | collective-permute-done | bytes 3670048 | tf_op jit(solution)/shard_map/ppermute | solution.py:12
  362.3 7.4 fusion.36
  369.8 14.1 %copy.17 = f32[64,8,64,128]{3,2,1,0:T(8,128)} copy(f32[64,8,64,128]{3,1,2,0:T(8,128)} %multiply_bitcast_fusion) | data formatting | bytes 33554432
  384.4 22.4 %fusion.211 = f32[512,128,64]{1,2,0:T(8,128)} fusion(f32[512,64,128]{2,1,0:T(8,128)} %bitcast.48, s32[64]{0:T(128)S(1)} %get-tuple-element.42, s32[64]{0:T(128)S(1)} %get-tuple-element.59, s32[64]{0:T(128)S(1)} %get-tuple-element.60, s32[64]{0:T(128)S(1)} %get-tuple-element.61, s32[64]{0:T(128)S(1)} %get-tuple-element.62, s32[64]{0:T(128)S(1)} %get-tuple-element.63, ...), kind=kOutput, calls=%fused_computation.313 | convolution fusion | flops 3221409792 | bytes 33558528 | tf_op jit(solution)/shard_map/ac,ncb->nab/dot_general | solution.py:37
  406.8 0.5 add_select_fusion.2
  407.3 1.6 collective-permute-start.5
  409.0 19.5 %fusion = f32[512,64,128]{2,1,0:T(8,128)} fusion(f32[512,128,64]{1,2,0:T(8,128)} %fusion.211, s32[128]{0:T(128)S(1)} %get-tuple-element.43, s32[128]{0:T(128)S(1)} %get-tuple-element.44, s32[128]{0:T(128)S(1)} %get-tuple-element.45, s32[128]{0:T(128)S(1)} %get-tuple-element.46, s32[128]{0:T(128)S(1)} %get-tuple-element.47, s32[128]{0:T(128)S(1)} %get-tuple-element.48, ...), kind=kOutput, calls=%fused_computation.1 | convolution fusion | flops 6443188224 | bytes 33562624 | tf_op jit(solution)/shard_map/bd,nad->nab/dot_general | solution.py:38
  428.5 23.1 %fusion.6 = f32[512,64,128]{2,1,0:T(8,128)} fusion(f32[512,64,128]{2,1,0:T(8,128)} %fusion, f32[64,128]{1,0:T(8,128)S(1)} %bitcast.51, s32[64]{0:T(128)S(1)} %get-tuple-element.42, s32[64]{0:T(128)S(1)} %get-tuple-element.59, s32[64]{0:T(128)S(1)} %get-tuple-element.60, s32[64]{0:T(128)S(1)} %get-tuple-element.61, s32[64]{0:T(128)S(1)} %get-tuple-element.62, ...), kind=kOutput, calls=%fused_computation.8 | convolution fusion | flops 3225604096 | bytes 33591296 | tf_op jit(solution)/shard_map/ac,ncb->nab/dot_general | solution.py:37
  451.6 33.7 %fusion.2 = f32[512,64,128]{0,2,1:T(8,128)} fusion(f32[512,64,128]{2,1,0:T(8,128)} %fusion.6, s32[128]{0:T(128)S(1)} %get-tuple-element.43, s32[128]{0:T(128)S(1)} %get-tuple-element.44, s32[128]{0:T(128)S(1)} %get-tuple-element.45, s32[128]{0:T(128)S(1)} %get-tuple-element.46, s32[128]{0:T(128)S(1)} %get-tuple-element.47, s32[128]{0:T(128)S(1)} %get-tuple-element.48, ...), kind=kOutput, calls=%fused_computation.3 | convolution fusion | flops 6443188224 | bytes 33562624 | tf_op jit(solution)/shard_map/bd,nad->nab/dot_general | solution.py:38
  485.3 3.8 collective-permute-done.5
  489.6 1.9 collective-permute-start.6
  491.4 11.4 %bitcast_multiply_fusion = f32[512,8192]{0,1:T(8,128)} fusion(f32[512,64,128]{0,2,1:T(8,128)} %fusion.2, f32[8192]{0:T(1024)S(1)} %bitcast.50), kind=kLoop, calls=%fused_computation | loop fusion | flops 4194304 | bytes 33587200 | tf_op jit(solution)/shard_map/mul | solution.py:99
  502.9 19.0 %fusion.50 = f32[512,64,1]{0,1,2:T(8,128)S(1)} fusion(f32[512,8192]{0,1:T(8,128)} %bitcast_multiply_fusion, s32[64]{0:T(128)S(1)} %get-tuple-element.38, s32[8192]{0:T(1024)S(1)} %get-tuple-element.73, s32[64]{0:T(128)S(1)} %get-tuple-element.30, s32[8192]{0:T(1024)S(1)} %get-tuple-element.74, s32[64]{0:T(128)S(1)} %get-tuple-element.34, ...), kind=kOutput, calls=%fused_computation.51 | convolution fusion | flops 3245342720 | bytes 17436672 | tf_op jit(solution)/shard_map/dot_general | solution.py:100
  521.9 48.8 %collective-permute-done.6 = f32[7,256,512]{1,2,0:T(8,128)S(1)} collective-permute-done((f32[7,256,512]{1,2,0:T(8,128)S(1)}, f32[7,256,512]{1,2,0:T(8,128)S(1)}, u32[]{:S(2)}, u32[]{:S(2)}) %collective-permute-start.6) | collective-permute-done | bytes 3670048 | tf_op jit(solution)/shard_map/ppermute | solution.py:12
  571.1 3.4 collective-permute-start.7
  574.5 23.0 %convolution_convert_fusion = bf16[1792,512]{1,0:T(8,128)(2,1)} fusion(bf16[1792,8192]{1,0:T(8,128)(2,1)} %bitcast.53, bf16[512,8192]{1,0:T(8,128)(2,1)} %param.9), kind=kOutput, calls=%fused_computation.32 | convolution fusion | flops 15033303040 | bytes 39583744 | tf_op jit(solution)/shard_map/dot_general | solution.py:68
  597.5 133.3 %collective-permute-done.7 = f32[7,256,512]{1,2,0:T(8,128)} collective-permute-done((f32[7,256,512]{1,2,0:T(8,128)S(1)}, f32[7,256,512]{1,2,0:T(8,128)}, u32[]{:S(2)}, u32[]{:S(2)}) %collective-permute-start.7) | collective-permute-done | bytes 3670048 | tf_op jit(solution)/shard_map/ppermute | solution.py:12
  730.8 7.0 fusion.47
  737.9 91.6 %all-reduce.2.cloned.1.call-done = f32[64,512]{1,0:T(8,128)} async-done(((f32[64,512]{1,0:T(8,128)}), f32[64,512]{1,0:T(8,128)}) %all-reduce.2.cloned.1.call-update) | async-done | bytes 131088 | tf_op jit(solution)/shard_map/psum | solution.py:93
  829.5 1.9 fusion.89
  831.4 0.6 constant_dynamic-slice_fusion
  (66 shorter events, 2.1 us)
Async XLA Ops:
  7.2 822.3 %all-reduce.2.cloned.1.call-start = ((), (), s32[]{:S(2)}) async-start(), calls=%async_computation | async-start | bytes 262144 | tf_op jit(solution)/shard_map/psum | solution.py:93
  18.0 6.8 collective-permute-start
  30.2 81.7 %collective-permute-start.1 = (f32[7,256,512]{1,2,0:T(8,128)}, f32[7,256,512]{1,2,0:T(8,128)}, u32[]{:S(2)}, u32[]{:S(2)}) collective-permute-start(f32[7,256,512]{1,2,0:T(8,128)} %add_select_fusion.5), channel_id=1, source_target_pairs={{0,2},{1,3},{2,0},{3,1},{4,6},{5,7},{6,4},{7,5},{8,10},{9,11},{10,... | collective-permute-start | bytes 11010056 | tf_op jit(solution)/shard_map/ppermute | solution.py:12
  31.8 85.9 %copy-start = (s32[3,8192]{1,0:T(4,128)S(1)}, s32[3,8192]{1,0:T(4,128)}, u32[]{:S(2)}) copy-start(s32[3,8192]{1,0:T(4,128)} %param.12) | copy-start | bytes 294916
  117.4 80.9 %collective-permute-start.2 = (f32[7,256,512]{1,2,0:T(8,128)}, f32[7,256,512]{1,2,0:T(8,128)}, u32[]{:S(2)}, u32[]{:S(2)}) collective-permute-start(f32[7,256,512]{1,2,0:T(8,128)} %add_select_fusion.4), channel_id=1, source_target_pairs={{0,4},{1,5},{2,6},{3,7},{4,0},{5,1},{6,2},{7,3},{8,12},{9,13},{10,... | collective-permute-start | bytes 11010056 | tf_op jit(solution)/shard_map/ppermute | solution.py:12
  203.7 158.6 %collective-permute-start.3 = (f32[7,256,512]{1,2,0:T(8,128)}, f32[7,256,512]{1,2,0:T(8,128)}, u32[]{:S(2)}, u32[]{:S(2)}) collective-permute-start(f32[7,256,512]{1,2,0:T(8,128)} %add_select_fusion.3), channel_id=1, source_target_pairs={{0,8},{1,9},{2,10},{3,11},{4,12},{5,13},{6,14},{7,15},{8,0},{9,1},... | collective-permute-start | bytes 11010056 | tf_op jit(solution)/shard_map/ppermute | solution.py:12
  369.7 37.1 %collective-permute-start.4 = (f32[7,256,512]{1,2,0:T(8,128)S(1)}, f32[7,256,512]{1,2,0:T(8,128)S(1)}, u32[]{:S(2)}, u32[]{:S(2)}) collective-permute-start(f32[7,256,512]{1,2,0:T(8,128)S(1)} %fusion.36), channel_id=1, source_target_pairs={{0,1},{1,0},{2,3},{3,2},{4,5},{5,4},{6,7},{7,6},{8,9},{9,8},{10,11... | collective-permute-start | bytes 11010056 | tf_op jit(solution)/shard_map/ppermute | solution.py:12
  369.8 14.5 %copy-start.2 = (s32[64]{0:T(128)S(1)}, s32[64]{0:T(128)}, u32[]{:S(2)}) copy-start(s32[64]{0:T(128)} %param.13) | copy-start | bytes 772
  369.8 14.5 %copy-start.1 = (s32[64]{0:T(128)S(1)}, s32[64]{0:T(128)}, u32[]{:S(2)}) copy-start(s32[64]{0:T(128)} %param.14) | copy-start | bytes 772
  407.3 81.8 %collective-permute-start.5 = (f32[7,256,512]{1,2,0:T(8,128)S(1)}, f32[7,256,512]{1,2,0:T(8,128)S(1)}, u32[]{:S(2)}, u32[]{:S(2)}) collective-permute-start(f32[7,256,512]{1,2,0:T(8,128)S(1)} %add_select_fusion.2), channel_id=1, source_target_pairs={{0,2},{1,3},{2,0},{3,1},{4,6},{5,7},{6,4},{7,5},{8,10},{9,11},{10,... | collective-permute-start | bytes 11010056 | tf_op jit(solution)/shard_map/ppermute | solution.py:12
  489.6 81.1 %collective-permute-start.6 = (f32[7,256,512]{1,2,0:T(8,128)S(1)}, f32[7,256,512]{1,2,0:T(8,128)S(1)}, u32[]{:S(2)}, u32[]{:S(2)}) collective-permute-start(f32[7,256,512]{1,2,0:T(8,128)S(1)} %add_select_fusion.1), channel_id=1, source_target_pairs={{0,4},{1,5},{2,6},{3,7},{4,0},{5,1},{6,2},{7,3},{8,12},{9,13},{10,... | collective-permute-start | bytes 11010056 | tf_op jit(solution)/shard_map/ppermute | solution.py:12
  571.1 159.6 %collective-permute-start.7 = (f32[7,256,512]{1,2,0:T(8,128)S(1)}, f32[7,256,512]{1,2,0:T(8,128)}, u32[]{:S(2)}, u32[]{:S(2)}) collective-permute-start(f32[7,256,512]{1,2,0:T(8,128)S(1)} %add_select_fusion), channel_id=1, source_target_pairs={{0,8},{1,9},{2,10},{3,11},{4,12},{5,13},{6,14},{7,15},{8,0},{9,1},... | collective-permute-start | bytes 11010056 | tf_op jit(solution)/shard_map/ppermute | solution.py:12
  730.8 7.0 copy-start.3
Sparse Core Ops, SparseCore 0:
  737.9 91.5 all-reduce.1
where the time goes:
time: 848 us; the launch traced here: 839 us
  waiting for transfers between devices  589 us (69%)
  matrix products  167 us (20%)
  other arithmetic  42.1 us (5%)
  local copies, waits for them, and re-layouts  14.9 us (2%)
  between operations  14.6 us (2%)
  starting transfers between devices  11.3 us (1%)
    ppermute x8, waiting for transfers between devices, from_partner(): lax.ppermute(array, axis, [(i, i ^ 1 << bit) for i in range(lax.axis_size...  498 us
    psum x1, waiting for transfers between devices, body(): hidden_proj = lax.psum(partial_proj, 'tensor')  91.6 us
    dot_general x2, matrix products, walsh_last(): jnp.einsum('bd,nad->nab', walsh_table(second_len), shaped, precision=high...  53.2 us
    dot_general x2, matrix products, walsh_last(): jnp.einsum('ac,ncb->nab', walsh_table(first_len), shaped, precision=highest)  45.6 us
    dot_general x1, matrix products, body(): lax.dot_general(flat_weight, out_grad, (((1,), (1,)), ((), ())), preferre...  23 us
    dot_general x1, matrix products, body(): grad_proj = jnp.dot(mixed_grad, final_table, precision=highest)  19 us
    select_n x6, other arithmetic, body(): mixed = jnp.where(upper, partner - mixed, mixed + partner)  17.8 us
    dot_general x2, matrix products, body(): mixed = jnp.einsum('ac,qct->qat', local_table, mixed, precision=highest)  17.4 us
  transfers between devices with their start and end apart: 9, of which 8 were waited for; matrix products, arithmetic and copies ran while one was open for 21% of the time, Pallas kernels for 0%

commit v1 on v0

v1 whole, which is shorter than its diff:
```python
import functools
import math

import jax
import jax.numpy as jnp
from jax import lax
from jax.experimental import pallas as pl
from jax.experimental.pallas import tpu as pltpu
from jax.sharding import PartitionSpec as P

highest = lax.Precision.HIGHEST
MB = 1 << 20
BLOCK = 256
BF, F32 = jnp.bfloat16, jnp.float32


def parity_sign(first_ids, second_ids):
    common = first_ids & second_ids
    for shift in (8, 4, 2, 1):
        common = common ^ (common >> shift)
    return (1 - 2 * (common & 1)).astype(F32)


def iota(shape, dim):
    return lax.broadcasted_iota(jnp.int32, shape, dim)


def table():
    return parity_sign(iota((BLOCK, BLOCK), 0), iota((BLOCK, BLOCK), 1)).astype(BF)


def dot(a, b):
    return jnp.dot(a, b, preferred_element_type=F32)


def dot_nt(a, b):
    return lax.dot_general(a, b, (((1,), (1,)), ((), ())), preferred_element_type=F32)


def two_terms(x):
    hi = x.astype(BF)
    return hi, (x - hi.astype(F32)).astype(BF)


def butterflies(blocks):
    blocks = list(blocks)
    step = 1
    while step < len(blocks):
        for i in range(len(blocks)):
            if not i & step:
                a, b = blocks[i], blocks[i + step]
                blocks[i], blocks[i + step] = a + b, a - b
        step *= 2
    return blocks


def hidden_kernel(n, picks_ref, signs_ref, x_ref, out_ref):
    blocks, rows, _ = x_ref.shape
    length = signs_ref.shape[2]
    parts = length // BLOCK
    sketch = picks_ref.shape[0]
    start = lax.axis_index("tensor") * rows
    home = start // BLOCK
    picks = picks_ref[...]
    pick_q = picks // length
    pick_r = picks % length
    chosen = (pick_q == iota((sketch, blocks), 1)).astype(BF)

    def sign_of(section, where):
        return 1.0 - 2.0 * dot(chosen, signs_ref[section, :, where].astype(F32).astype(BF))

    walsh = table()
    low = parity_sign(pick_r % BLOCK, iota((sketch, BLOCK), 1))
    high = pick_r // BLOCK
    first = []
    for c in range(parts):
        where = pl.ds(c * BLOCK, BLOCK)
        v = low * parity_sign(high, jnp.full_like(high, c)) * sign_of(2, where)
        first.append(dot(v.astype(BF), walsh))
    first = butterflies(first)
    total = None
    for c in range(parts):
        side = parity_sign(jnp.full((1, BLOCK), home, jnp.int32), jnp.full((1, BLOCK), c, jnp.int32))
        term = first[c] * (sign_of(1, pl.ds(c * BLOCK, BLOCK)) * side)
        total = term if total is None else total + term
    hi, lo = two_terms(total)
    second = dot(hi, walsh) + dot(lo, walsh)
    second = second * sign_of(0, pl.ds(pl.multiple_of(home * BLOCK, BLOCK), BLOCK))
    hi, lo = two_terms(second)
    if rows < BLOCK:
        pick_out = (iota((BLOCK, rows), 0) == iota((BLOCK, rows), 1) + (start - home * BLOCK)).astype(F32).astype(BF)
        hi = dot(hi, pick_out).astype(BF)
        lo = dot(lo, pick_out).astype(BF)
    total = None
    for q in range(blocks):
        own = pick_q == q
        both = jnp.concatenate([jnp.where(own, hi.astype(F32), 0.0), jnp.where(own, lo.astype(F32), 0.0)], axis=0)
        term = dot(both.astype(BF), x_ref[q])
        total = term if total is None else total + term
    out_ref[...] = (total[:sketch] + total[sketch:]) * (length ** -1.5)


def main_kernel(steps, picks_ref, signs_ref, w_ref, g_hbm, out_ref, proj_ref, g_vm, acc, sketcher, sems):
    i = pl.program_id(0)
    width = g_hbm.shape[1]
    tile = width // steps
    parts = width // BLOCK

    def fetch(j):
        return pltpu.make_async_copy(
            g_hbm.at[:, pl.ds(pl.multiple_of(j * tile, tile), tile)], g_vm.at[j], sems.at[j]
        )

    @pl.when(i == 0)
    def _():
        fetch(0).start()
        acc[...] = jnp.zeros_like(acc)

    @pl.when(i < steps - 1)
    def _():
        fetch(i + 1).start()

    fetch(i).wait()
    picks = picks_ref[pl.ds(pl.multiple_of(i * 8, 8), 8), :]
    walsh = table()
    low = parity_sign(picks % BLOCK, iota((8, BLOCK), 1))
    high = picks // BLOCK

    def sign_of(section, c):
        bits = signs_ref[section : section + 1, c * BLOCK : (c + 1) * BLOCK]
        return (1 - 2 * bits).astype(F32)

    def rows_of(x, c):
        return x[c * 8 : (c + 1) * 8]

    v = [low * parity_sign(high, jnp.full_like(high, c)) * sign_of(2, c) for c in range(parts)]
    first = dot(jnp.concatenate(v, axis=0).astype(BF), walsh)
    first = butterflies([rows_of(first, c) for c in range(parts)])
    first = jnp.concatenate([first[c] * sign_of(1, c) for c in range(parts)], axis=0)
    hi, lo = two_terms(first)
    second = dot(hi, walsh) + dot(lo, walsh)
    second = butterflies([rows_of(second, c) for c in range(parts)])
    for c in range(parts):
        x = second[c] * sign_of(0, c)
        h = x.astype(BF).astype(F32)
        both = jnp.concatenate([h, x - h], axis=0).astype(BF)
        at = c * BLOCK // tile
        sketcher[at, pl.ds(pl.multiple_of(i * 16, 16), 16), c * BLOCK - at * tile : (c + 1) * BLOCK - at * tile] = both
    acc[...] += dot_nt(w_ref[...], g_vm[i])

    @pl.when(i == steps - 1)
    def _():
        out_ref[...] = acc[...].astype(BF)
        total = dot_nt(sketcher[0], g_vm[0])
        for j in range(1, steps):
            total = total + dot_nt(sketcher[j], g_vm[j])
        for j in range(steps):
            proj_ref[j * 8 : (j + 1) * 8, :] = (total[j * 16 : j * 16 + 8] + total[j * 16 + 8 : j * 16 + 16]) * (
                width ** -1.5
            )


def make_mask(positions, seq_lengths, seq_len):
    owner_seq = positions // seq_len
    seq_ids = jnp.arange(seq_lengths.shape[0], dtype=jnp.int32)
    inside = (positions % seq_len)[None, :] < seq_lengths[:, None]
    return ((owner_seq[None, :] == seq_ids[:, None]) & inside).astype(F32)


def body(hidden_in, out_grad, down_weight, hidden_signs, grad_signs, hidden_picks, grad_picks, seq_lengths):
    n = lax.axis_size("tensor")
    rank = lax.axis_index("tensor")
    blocks, rows, tokens = hidden_in.shape
    width = out_grad.shape[1]
    sketch = hidden_picks.shape[0]
    seqs = seq_lengths.shape[0]
    seq_len = tokens // seqs
    vmem = pl.BlockSpec(memory_space=pltpu.VMEM)
    partial = pl.pallas_call(
        functools.partial(hidden_kernel, n),
        out_shape=jax.ShapeDtypeStruct((sketch, tokens), F32),
        in_specs=[vmem] * 3,
        out_specs=vmem,
        compiler_params=pltpu.CompilerParams(vmem_limit_bytes=32 * MB),
        cost_estimate=pl.CostEstimate(flops=10**9, bytes_accessed=4 * 10**6, transcendentals=0),
    )(hidden_picks.reshape(sketch, 1), hidden_signs, hidden_in)
    scatter = sketch % n == 0
    if scatter:
        hidden_proj = lax.psum_scatter(partial, "tensor", scatter_dimension=0, tiled=True)
    else:
        hidden_proj = lax.psum(partial, "tensor")

    steps = sketch // 8
    tile = width // steps
    m = blocks * rows
    flat_weight = down_weight.reshape(m, width)
    input_grad, grad_proj = pl.pallas_call(
        functools.partial(main_kernel, steps),
        grid=(steps,),
        out_shape=(jax.ShapeDtypeStruct((m, tokens), BF), jax.ShapeDtypeStruct((sketch, tokens), F32)),
        in_specs=[
            pl.BlockSpec((sketch, 1), lambda i: (0, 0)),
            pl.BlockSpec(grad_signs.shape, lambda i: (0, 0)),
            pl.BlockSpec((m, tile), lambda i: (0, i)),
            pl.BlockSpec(memory_space=pl.ANY),
        ],
        out_specs=(pl.BlockSpec((m, tokens), lambda i: (0, 0)), pl.BlockSpec((sketch, tokens), lambda i: (0, 0))),
        scratch_shapes=[
            pltpu.VMEM((steps, tokens, tile), BF),
            pltpu.VMEM((m, tokens), F32),
            pltpu.VMEM((steps, 2 * sketch, tile), BF),
            pltpu.SemaphoreType.DMA((steps,)),
        ],
        compiler_params=pltpu.CompilerParams(vmem_limit_bytes=48 * MB, dimension_semantics=("arbitrary",)),
        cost_estimate=pl.CostEstimate(
            flops=2 * (m + 2 * sketch) * tokens * width, bytes_accessed=2 * (m + tokens) * width, transcendentals=0
        ),
    )(grad_picks.reshape(sketch, 1), grad_signs, flat_weight, out_grad)
    input_grad = input_grad.reshape(blocks, rows, tokens)

    share = sketch * sketch // n
    live = make_mask(jnp.arange(tokens, dtype=jnp.int32), seq_lengths, seq_len)
    live = live.reshape(seqs, seqs, seq_len).sum(axis=0)
    left = hidden_proj.reshape(-1, seqs, seq_len) * live[None]
    right = grad_proj.reshape(sketch, seqs, seq_len)
    found = jnp.einsum("ast,bst->sab", left, right, precision=highest).reshape(seqs, -1)
    if not scatter:
        found = lax.dynamic_slice_in_dim(found, rank * share, share, 1)
    return (input_grad, found)


def solution(mesh):
    in_specs = (
        P(None, "tensor", "groups"),
        P("groups", None),
        P(None, "tensor", None),
        P(),
        P(),
        P(),
        P(),
        P("groups"),
    )
    out_specs = (P(None, "tensor", "groups"), P("groups", "tensor"))
    return jax.shard_map(body, mesh=mesh, in_specs=in_specs, out_specs=out_specs, check_vma=False)
```

time: 848 us -> 114 us (0.13); the launches traced: 839 us -> 114 us
  waiting for transfers between devices: 589 us -> 59 us
  matrix products: 167 us -> 0.52 us
  other arithmetic: 42.1 us -> 0.09 us
  Pallas kernels: 0 us -> 32.3 us
  starting transfers between devices: 11.3 us -> 0.04 us
    ppermute x8 -> x0, waiting for transfers between devices: 498 us -> none  [from_partner(): lax.ppermute(array, axis, [(i, i ^ 1 << bit) for i in range(lax.axis_size...]
    dot_general x10 -> x1, matrix products: 167 us -> 0.52 us  [body(): jnp.einsum('ast,bst->sab', left, right, precision=highest).reshape(seqs, -1)]
    psum x1 -> x0, waiting for transfers between devices: 91.6 us -> none  [body(): hidden_proj = lax.psum(partial_proj, 'tensor')]
    unnamed x1 -> x2, waiting for transfers between devices: 0.02 us -> 59 us
    pallas_call x0 -> x2, Pallas kernels: none -> 32.3 us  [the longest x1 28.7 us: body(): pl.pallas_call(functools.partial(main_kernel, steps), grid=(steps,), out_...]
    select_n x49 -> x0, other arithmetic: 18.2 us -> none  [the longest x6 17.8 us: body(): mixed = jnp.where(upper, partner - mixed, mixed + partner)]
    mul x2 -> x0, other arithmetic: 11.5 us -> none  [body(): mixed_grad = walsh_last(mixed_grad, width) * grad_sign[2][None, :]]
    unnamed x1 -> x0, other arithmetic: 11.4 us -> none
  transfers between devices with their start and end apart: 9 -> 1, of which waited for: 8 -> 1; matrix products, arithmetic and copies ran while one was open for 21% -> 1% of each run, Pallas kernels for 0% -> 25%
where the time goes in v1:
time: 114 us
  waiting for transfers between devices  59 us (52%)
  Pallas kernels  32.3 us (28%)
  between operations  14.7 us (13%)
  local copies, waits for them, and re-layouts  7.08 us (6%)
    unnamed x2, waiting for transfers between devices  59 us
    pallas_call x1, Pallas kernels, body(): pl.pallas_call(functools.partial(main_kernel, steps), grid=(steps,), out_...  28.7 us
    unnamed x12, local copies, waits for them, and re-layouts  4.71 us
    pallas_call x1, Pallas kernels, body(): pl.pallas_call(functools.partial(hidden_kernel, n), out_shape=jax.ShapeDt...  3.61 us
  transfers between devices with their start and end apart: 1, of which 1 were waited for; matrix products, arithmetic and copies ran while one was open for 1% of the time, Pallas kernels for 25%

profile of v1, /device:TPU:8, one launch (start us, length us, event | category | flops | bytes accessed | tf_op | source)
XLA Modules:
  0.0 113.8 jit_solution(17168905270622670021)
XLA Ops:
  7.2 0.0 all-reduce.3.cloned.1.call-start
  7.2 0.7 copy.19.picks_ref
  8.0 0.0 copy-start
  8.0 1.5 %copy-done = bf16[7,256,512]{2,1,0:T(8,128)(2,1)S(1)} copy-done((bf16[7,256,512]{2,1,0:T(8,128)(2,1)S(1)}, bf16[7,256,512]{2,1,0:T(8,128)(2,1)}, u32[]{:S(2)}) %copy-start) | copy-done | bytes 1835032
  9.5 0.0 copy-start.1
  9.5 1.0 copy-done.1
  10.5 3.6 %shard_map.96 = f32[64,512]{1,0:T(8,128)} custom-call(s32[64,1]{1,0:T(8,128)S(1)} %copy.19.picks_ref, s32[3,7,4096]{2,1,0:T(8,128)S(1)} %copy-done.1, bf16[7,256,512]{2,1,0:T(8,128)(2,1)S(1)} %copy-done), custom_call_target="tpu_custom_call" | custom-call | flops 1000000000 | bytes 4000000 | tf_op jit(solution)/shard_map/pallas_call | solution.py:179
  14.1 0.0 all-reduce.3.cloned.1.call-update
  14.1 0.7 copy.18.picks_ref
  14.9 0.0 copy-start.2
  14.9 0.9 copy-done.2
  15.8 0.0 copy-start.4
  15.8 0.0 copy-start.3
  15.8 28.7 %shard_map.95 = (bf16[1792,512]{1,0:T(8,128)(2,1)}, f32[64,512]{1,0:T(8,128)S(1)}) custom-call(s32[64,1]{1,0:T(8,128)S(1)} %copy.18.picks_ref, s32[3,8192]{1,0:T(4,128)S(1)} %copy-done.2, bf16[1792,8192]{1,0:T(8,128)(2,1)} %bitcast.7, bf16[512,8192]{1,0:T(8,128)(2,1)} %g_hbm.1), custom_call_target="tpu_custom_call" | custom-call | flops 16106127360 | bytes 37748736 | tf_op jit(solution)/shard_map/pallas_call | solution.py:197
  44.5 0.1 reshape.75
  44.6 0.0 copy-done.4
  44.6 0.6 dynamic-slice
  45.9 0.0 copy-done.3
  45.9 0.1 convert_reduce_fusion
  45.9 59.0 %all-reduce.3.cloned.1.call-done = f32[64,512]{1,0:T(8,128)} async-done(((f32[64,512]{1,0:T(8,128)}), f32[64,512]{1,0:T(8,128)}) %all-reduce.3.cloned.1.call-update) | async-done | bytes 131088
  104.9 0.7 constant_dynamic-slice_fusion
  105.6 0.1 reshape.74
  105.7 0.5 fusion
  106.2 0.7 reshape.76
  (1 shorter events, 0.0 us)
Async XLA Ops:
  7.2 97.7 %all-reduce.3.cloned.1.call-start = ((), (), s32[]{:S(2)}) async-start(), calls=%async_computation | async-start | bytes 262144
  8.0 1.5 %copy-start = (bf16[7,256,512]{2,1,0:T(8,128)(2,1)S(1)}, bf16[7,256,512]{2,1,0:T(8,128)(2,1)}, u32[]{:S(2)}) copy-start(bf16[7,256,512]{2,1,0:T(8,128)(2,1)} %x_ref.1) | copy-start | bytes 5505028
  9.5 1.0 copy-start.1
  14.9 0.9 copy-start.2
  15.8 28.8 %copy-start.4 = (u32[32]{0:T(128)S(1)}, u32[32]{0:T(128)}, u32[]{:S(2)}) copy-start(u32[32]{0:T(128)} %constant.39) | copy-start | bytes 388
  15.8 30.1 %copy-start.3 = (s32[8]{0:T(128)S(1)}, s32[8]{0:T(128)}, u32[]{:S(2)}) copy-start(s32[8]{0:T(128)} %param.15) | copy-start | bytes 100
Sparse Core Ops, SparseCore 0:
  14.2 90.6 all-reduce.2

commit v2 on v1

v2 whole, which is shorter than its diff:
```python
import functools

import jax
import jax.numpy as jnp
from jax import lax
from jax.experimental import pallas as pl
from jax.experimental.pallas import tpu as pltpu
from jax.sharding import PartitionSpec as P

highest = lax.Precision.HIGHEST
MB = 1 << 20
BLOCK = 256
BF, F32 = jnp.bfloat16, jnp.float32


def parity_sign(first_ids, second_ids):
    common = first_ids & second_ids
    for shift in (8, 4, 2, 1):
        common = common ^ (common >> shift)
    return (1 - 2 * (common & 1)).astype(F32)


def iota(shape, dim):
    return lax.broadcasted_iota(jnp.int32, shape, dim)


def table():
    return parity_sign(iota((BLOCK, BLOCK), 0), iota((BLOCK, BLOCK), 1)).astype(BF)


def dot(a, b):
    return jnp.dot(a, b, preferred_element_type=F32)


def dot_nt(a, b):
    return lax.dot_general(a, b, (((1,), (1,)), ((), ())), preferred_element_type=F32)


def two_terms(x):
    hi = x.astype(BF)
    return hi, (x - hi.astype(F32)).astype(BF)


def butterflies(blocks):
    blocks = list(blocks)
    step = 1
    while step < len(blocks):
        for i in range(len(blocks)):
            if not i & step:
                a, b = blocks[i], blocks[i + step]
                blocks[i], blocks[i + step] = a + b, a - b
        step *= 2
    return blocks


def column(row, base, count):
    shape = (count, row.shape[1])
    wanted = iota(shape, 1) == iota(shape, 0) + base
    return jnp.sum(jnp.where(wanted, row.astype(F32), 0.0), axis=1, keepdims=True).astype(jnp.int32)


def hidden_share(me, picks, signs_ref, shape):
    blocks, rows, _ = shape
    length = signs_ref.shape[2]
    parts = length // BLOCK
    sketch = picks.shape[0]
    start = me * rows
    home = start // BLOCK
    pick_q = picks // length
    pick_r = picks % length
    chosen = (pick_q == iota((sketch, blocks), 1)).astype(F32).astype(BF)

    def sign_of(section, where):
        return 1.0 - 2.0 * dot(chosen, signs_ref[section, :, where].astype(F32).astype(BF))

    walsh = table()
    low = parity_sign(pick_r % BLOCK, iota((sketch, BLOCK), 1))
    high = pick_r // BLOCK
    first = []
    for c in range(parts):
        v = low * parity_sign(high, jnp.full_like(high, c)) * sign_of(2, pl.ds(c * BLOCK, BLOCK))
        first.append(dot(v.astype(BF), walsh))
    first = butterflies(first)
    total = None
    for c in range(parts):
        side = parity_sign(jnp.full((1, BLOCK), home, jnp.int32), jnp.full((1, BLOCK), c, jnp.int32))
        term = first[c] * (sign_of(1, pl.ds(c * BLOCK, BLOCK)) * side)
        total = term if total is None else total + term
    hi, lo = two_terms(total)
    second = dot(hi, walsh) + dot(lo, walsh)
    second = second * sign_of(0, pl.ds(pl.multiple_of(home * BLOCK, BLOCK), BLOCK))
    hi, lo = two_terms(second)
    if rows < BLOCK:
        pick_out = (iota((BLOCK, rows), 0) == iota((BLOCK, rows), 1) + (start - home * BLOCK)).astype(F32).astype(BF)
        hi = dot(hi, pick_out).astype(BF)
        lo = dot(lo, pick_out).astype(BF)
    return pick_q, hi, lo


def grad_share(picks, signs_ref, write):
    width = signs_ref.shape[1]
    parts = width // BLOCK
    walsh = table()
    low = parity_sign(picks % BLOCK, iota((8, BLOCK), 1))
    high = picks // BLOCK

    def sign_of(section, c):
        bits = signs_ref[section : section + 1, c * BLOCK : (c + 1) * BLOCK]
        return (1 - 2 * bits).astype(F32)

    def rows_of(x, c):
        return x[c * 8 : (c + 1) * 8]

    v = [low * parity_sign(high, jnp.full_like(high, c)) * sign_of(2, c) for c in range(parts)]
    first = dot(jnp.concatenate(v, axis=0).astype(BF), walsh)
    first = butterflies([rows_of(first, c) for c in range(parts)])
    first = jnp.concatenate([first[c] * sign_of(1, c) for c in range(parts)], axis=0)
    hi, lo = two_terms(first)
    second = dot(hi, walsh) + dot(lo, walsh)
    second = butterflies([rows_of(second, c) for c in range(parts)])
    for c in range(parts):
        x = second[c] * sign_of(0, c)
        h = x.astype(BF).astype(F32)
        write(c, jnp.concatenate([h, x - h], axis=0).astype(BF))


def kernel(
    n, keep, hp_ref, gp_ref, len_ref, hs_hbm, gs_hbm, x_hbm, g_hbm, w_hbm, out_hbm, sk_ref,
    hs_vm, gs_vm, x_vm, g_vm, w_first, w_vm, o_vm, part, send, recv, in_sem, g_sem, w_sem, out_sem, send_sem, recv_sem,
):
    me = lax.axis_index("tensor")
    width = g_hbm.shape[1]
    tiles, bm, tokens = o_vm.shape
    blocks = x_hbm.shape[0]
    length = hs_hbm.shape[2]
    sketch = hp_ref.shape[1]
    pieces = sketch // keep
    seqs = len_ref.shape[1]
    seq_len = tokens // seqs
    g_parts = g_sem.shape[0]
    g_rows = tokens // g_parts

    def fetch_w(t, slot):
        where = pl.ds(pl.multiple_of(t * bm, bm), bm)
        return pltpu.make_async_copy(w_hbm.at[where, :], w_vm.at[slot], w_sem.at[slot + 1])

    def put_out(t):
        where = pl.ds(pl.multiple_of(t * bm, bm), bm)
        return pltpu.make_async_copy(o_vm.at[t], out_hbm.at[where, :], out_sem.at[t])

    def send_to(d):
        peer = lax.rem(me + d, n)
        return pltpu.make_async_remote_copy(
            src_ref=send.at[peer * pieces // n],
            dst_ref=recv.at[me],
            send_sem=send_sem.at[d],
            recv_sem=recv_sem.at[me],
            device_id={"tensor": peer},
            device_id_type=pl.DeviceIdType.MESH,
        )

    signs = [
        pltpu.make_async_copy(gs_hbm, gs_vm, in_sem.at[0]),
        pltpu.make_async_copy(hs_hbm, hs_vm, in_sem.at[1]),
    ]
    get_x = pltpu.make_async_copy(x_hbm, x_vm, in_sem.at[2])
    get_g = [
        pltpu.make_async_copy(g_hbm.at[pl.ds(j * g_rows, g_rows), :], g_vm.at[pl.ds(j * g_rows, g_rows), :], g_sem.at[j])
        for j in range(g_parts)
    ]
    get_w = pltpu.make_async_copy(w_hbm.at[pl.ds(0, bm), :], w_first.at[pl.ds(0, bm), :], w_sem.at[0])
    for copy in signs + [get_x] + get_g + [get_w]:
        copy.start()
    for t in range(1, min(3, tiles)):
        fetch_w(t, t - 1).start()

    barrier = pltpu.get_barrier_semaphore()

    def greet(d, carry):
        pl.semaphore_signal(
            barrier, inc=1, device_id={"tensor": lax.rem(me + d, n)}, device_id_type=pl.DeviceIdType.MESH
        )
        return carry

    lax.fori_loop(1, n, greet, 0)

    signs[0].wait()

    def write(c, both):
        w_first[bm : bm + 16, c * BLOCK : (c + 1) * BLOCK] = both

    grad_share(column(gp_ref[...], me * pieces // n * keep, 8), gs_vm, write)
    signs[1].wait()
    pick_q, hi, lo = hidden_share(me, column(hp_ref[...], 0, sketch), hs_vm, x_hbm.shape)
    get_x.wait()
    total = None
    for q in range(blocks):
        own = pick_q == q
        both = jnp.concatenate([jnp.where(own, hi.astype(F32), 0.0), jnp.where(own, lo.astype(F32), 0.0)], axis=0)
        term = dot(both.astype(BF), x_vm[q])
        total = term if total is None else total + term
    part[...] = (total[:sketch] + total[sketch:]) * (length ** -1.5)
    for copy in get_g:
        copy.wait()
    get_w.wait()

    tall = dot_nt(w_first[...], g_vm[...])
    o_vm[0] = tall[:bm].astype(BF)
    put_out(0).start()
    own_grad = (tall[bm : bm + 8] + tall[bm + 8 : bm + 16]) * (width ** -1.5)
    rest = send.shape[1] - 2 * keep
    for p in range(pieces):
        rows = [part[p * keep : (p + 1) * keep, :], own_grad[:keep]]
        if rest:
            rows.append(jnp.zeros((rest, tokens), F32))
        send[p] = jnp.concatenate(rows, axis=0)
    recv[me] = send[me * pieces // n]
    pl.semaphore_wait(barrier, n - 1)

    def start_send(d, carry):
        send_to(d).start()
        return carry

    lax.fori_loop(1, n, start_send, 0)

    def one_tile(t, carry):
        slot = lax.rem(t - 1, 2)
        fetch_w(t, slot).wait()
        o_vm[t] = dot_nt(w_vm[slot], g_vm[...]).astype(BF)
        put_out(t).start()

        @pl.when(t + 2 < tiles)
        def _():
            fetch_w(t + 2, slot).start()

        return carry

    if tiles > 1:
        lax.fori_loop(1, tiles, one_tile, 0)

    def end_send(d, carry):
        send_to(d).wait_send()
        peer = lax.rem(me + d, n)
        pltpu.make_async_remote_copy(
            src_ref=send.at[0],
            dst_ref=recv.at[peer],
            send_sem=send_sem.at[d],
            recv_sem=recv_sem.at[peer],
            device_id={"tensor": peer},
            device_id_type=pl.DeviceIdType.MESH,
        ).wait_recv()
        return carry

    lax.fori_loop(1, n, end_send, 0)
    found = recv[0][:keep]
    for j in range(1, n):
        found = found + recv[j][:keep]
    grads = jnp.concatenate([recv[p * n // pieces][keep : 2 * keep] for p in range(pieces)], axis=0)
    lens = column(len_ref[...], 0, seqs)
    places = iota((seqs, tokens), 1)
    live = ((places // seq_len == iota((seqs, tokens), 0)) & (places % seq_len < lens)).astype(F32)
    left = jnp.concatenate([live * found[a : a + 1] for a in range(keep)], axis=0)
    result = lax.dot_general(
        left, grads, (((1,), (1,)), ((), ())), precision=highest, preferred_element_type=F32
    )
    sk_ref[...] = jnp.concatenate([result[a * seqs : (a + 1) * seqs] for a in range(keep)], axis=1)

    def end_out(t, carry):
        put_out(t).wait()
        return carry

    lax.fori_loop(0, tiles, end_out, 0)


def body(hidden_in, out_grad, down_weight, hidden_signs, grad_signs, hidden_picks, grad_picks, seq_lengths):
    n = lax.axis_size("tensor")
    rank = lax.axis_index("tensor")
    blocks, rows, tokens = hidden_in.shape
    width = out_grad.shape[1]
    sketch = hidden_picks.shape[0]
    seqs = seq_lengths.shape[0]
    share = sketch * sketch // n
    keep = max(1, sketch // n)
    m = blocks * rows
    bm = BLOCK if m % BLOCK == 0 else m
    tiles = m // bm
    message = -(-2 * keep // 8) * 8
    flat_weight = down_weight.reshape(m, width)
    vmem = pl.BlockSpec(memory_space=pltpu.VMEM)
    hbm = pl.BlockSpec(memory_space=pl.ANY)
    dma = pltpu.SemaphoreType.DMA
    input_grad, example_sketch = pl.pallas_call(
        functools.partial(kernel, n, keep),
        out_shape=(
            jax.ShapeDtypeStruct((m, tokens), BF),
            jax.ShapeDtypeStruct((seqs, keep * sketch), F32),
        ),
        in_specs=[vmem] * 3 + [hbm] * 5,
        out_specs=(hbm, vmem),
        scratch_shapes=[
            pltpu.VMEM(hidden_signs.shape, jnp.int32),
            pltpu.VMEM(grad_signs.shape, jnp.int32),
            pltpu.VMEM(hidden_in.shape, BF),
            pltpu.VMEM((tokens, width), BF),
            pltpu.VMEM((bm + 16, width), BF),
            pltpu.VMEM((2, bm, width), BF),
            pltpu.VMEM((tiles, bm, tokens), BF),
            pltpu.VMEM((sketch, tokens), F32),
            pltpu.VMEM((sketch // keep, message, tokens), F32),
            pltpu.VMEM((n, message, tokens), F32),
            dma((3,)),
            dma((4,)),
            dma((3,)),
            dma((tiles,)),
            dma((n,)),
            dma((n,)),
        ],
        compiler_params=pltpu.CompilerParams(
            vmem_limit_bytes=56 * MB, collective_id=0, has_side_effects=True
        ),
        cost_estimate=pl.CostEstimate(
            flops=2 * m * tokens * width, bytes_accessed=2 * (m + tokens) * width, transcendentals=0
        ),
    )(
        hidden_picks.reshape(1, sketch),
        grad_picks.reshape(1, sketch),
        seq_lengths.reshape(1, seqs),
        hidden_signs,
        grad_signs,
        hidden_in,
        out_grad,
        flat_weight,
    )
    if share < keep * sketch:
        example_sketch = lax.dynamic_slice_in_dim(example_sketch, rank * share % sketch, share, 1)
    return (input_grad.reshape(blocks, rows, tokens), example_sketch)


def solution(mesh):
    in_specs = (
        P(None, "tensor", "groups"),
        P("groups", None),
        P(None, "tensor", None),
        P(),
        P(),
        P(),
        P(),
        P("groups"),
    )
    out_specs = (P(None, "tensor", "groups"), P("groups", "tensor"))
    return jax.shard_map(body, mesh=mesh, in_specs=in_specs, out_specs=out_specs, check_vma=False)
```

time: 114 us -> 30.4 us (0.27)
  waiting for transfers between devices: 59 us -> 0 us
  between operations: 14.7 us -> 0.65 us
  Pallas kernels: 32.3 us -> 26 us
  local copies, waits for them, and re-layouts: 7.08 us -> 3.51 us
    unnamed x2 -> x0, waiting for transfers between devices: 59 us -> none
    pallas_call x2 -> x1, Pallas kernels: 32.3 us -> 26 us  [body(): pl.pallas_call(functools.partial(kernel, n, keep), out_shape=(jax.ShapeDt...]
    reshape x5 -> x0, local copies, waits for them, and re-layouts: 2.37 us -> none  [the longest x1 0.75 us: body(): grad_picks.reshape(sketch, 1)]
    unnamed x12 -> x4, local copies, waits for them, and re-layouts: 4.71 us -> 3.51 us
  transfers between devices with their start and end apart: 1 -> 0, of which waited for: 1 -> 0; matrix products, arithmetic and copies ran while one was open for 1% -> 0% of each run, Pallas kernels for 25% -> 0%
where the time goes in v2:
time: 30.4 us; the launch traced here: 30.2 us
  Pallas kernels  26 us (86%)
  local copies, waits for them, and re-layouts  3.51 us (12%)
  between operations  0.65 us (2%)
    pallas_call x1, Pallas kernels, body(): pl.pallas_call(functools.partial(kernel, n, keep), out_shape=(jax.ShapeDt...  26 us
    unnamed x4, local copies, waits for them, and re-layouts  3.51 us

profile of v2, /device:TPU:8, one launch (start us, length us, event | category | flops | bytes accessed | tf_op | source)
XLA Modules:
  0.0 30.2 jit_solution(2367284686983229965)
XLA Ops:
  0.6 26.0 %shard_map.95 = (bf16[1792,512]{1,0:T(8,128)(2,1)}, f32[8,256]{1,0:T(8,128)}) custom-call(s32[1,64]{1,0:T(1,128)} %bitcast.7, s32[1,64]{1,0:T(1,128)} %bitcast.8, s32[1,8]{1,0:T(1,128)} %bitcast.9, s32[3,7,4096]{2,1,0:T(8,128)} %hs_hbm.1, s32[3,8192]{1,0:T(4,128)} %gs_hbm.1, bf16[7,256,512]{2,1,0:T(8,128)(2,1)} %x_hbm.1, bf16[512,8192]{1,0:T(8,128)(2,1)} %g_hbm.1, ...), custom_call_target="tpu_custom_call" | custom-call | flops 15032385536 | bytes 37748736 | tf_op jit(solution)/shard_map/pallas_call | solution.py:292
  26.7 0.0 copy-start
  26.7 2.9 %copy.12 = bf16[7,256,512]{2,1,0:T(8,128)(2,1)} copy(bf16[7,256,512]{2,1,0:T(8,128)(2,1)} %bitcast.5) | data formatting | bytes 3670016
  29.6 0.0 copy-done
  29.6 0.6 %copy.13 = f32[8,256]{1,0:T(8,128)} copy(f32[8,256]{1,0:T(8,128)S(1)} %copy-done) | data formatting | bytes 16384
Async XLA Ops:
  26.7 2.9 %copy-start = (f32[8,256]{1,0:T(8,128)S(1)}, f32[8,256]{1,0:T(8,128)}, u32[]{:S(2)}) copy-start(f32[8,256]{1,0:T(8,128)} %get-tuple-element.9) | copy-start | bytes 24580

commit v3 on v2

--- a/solution.py
+++ b/solution.py
@@ -125,8 +125,8 @@
 
 
 def kernel(
-    n, keep, hp_ref, gp_ref, len_ref, hs_hbm, gs_hbm, x_hbm, g_hbm, w_hbm, out_hbm, sk_ref,
-    hs_vm, gs_vm, x_vm, g_vm, w_first, w_vm, o_vm, part, send, recv, in_sem, g_sem, w_sem, out_sem, send_sem, recv_sem,
+    n, keep, hp_ref, gp_ref, hs_hbm, gs_hbm, x_hbm, g_hbm, w_hbm, out_hbm, found_ref, grads_ref,
+    hs_vm, gs_vm, x_vm, g_vm, w_first, w_vm, o_vm, part, send, recv, in_sem, g_sem, first_sem, w_sem, out_sem, send_sem, recv_sem,
 ):
     me = lax.axis_index("tensor")
     width = g_hbm.shape[1]
@@ -135,14 +135,12 @@
     length = hs_hbm.shape[2]
     sketch = hp_ref.shape[1]
     pieces = sketch // keep
-    seqs = len_ref.shape[1]
-    seq_len = tokens // seqs
-    g_parts = g_sem.shape[0]
-    g_rows = tokens // g_parts
+    chunks = g_sem.shape[0]
+    span = width // chunks
 
     def fetch_w(t, slot):
         where = pl.ds(pl.multiple_of(t * bm, bm), bm)
-        return pltpu.make_async_copy(w_hbm.at[where, :], w_vm.at[slot], w_sem.at[slot + 1])
+        return pltpu.make_async_copy(w_hbm.at[where, :], w_vm.at[slot], w_sem.at[slot])
 
     def put_out(t):
         where = pl.ds(pl.multiple_of(t * bm, bm), bm)
@@ -164,15 +162,23 @@
         pltpu.make_async_copy(hs_hbm, hs_vm, in_sem.at[1]),
     ]
     get_x = pltpu.make_async_copy(x_hbm, x_vm, in_sem.at[2])
-    get_g = [
-        pltpu.make_async_copy(g_hbm.at[pl.ds(j * g_rows, g_rows), :], g_vm.at[pl.ds(j * g_rows, g_rows), :], g_sem.at[j])
-        for j in range(g_parts)
-    ]
-    get_w = pltpu.make_async_copy(w_hbm.at[pl.ds(0, bm), :], w_first.at[pl.ds(0, bm), :], w_sem.at[0])
-    for copy in signs + [get_x] + get_g + [get_w]:
+    early = []
+    for j in range(chunks):
+        where = pl.ds(j * span, span)
+        early.append(
+            (
+                pltpu.make_async_copy(g_hbm.at[:, where], g_vm.at[:, where], g_sem.at[j]),
+                pltpu.make_async_copy(
+                    w_hbm.at[pl.ds(0, bm), where], w_first.at[pl.ds(0, bm), where], first_sem.at[j]
+                ),
+            )
+        )
+    for copy in signs:
         copy.start()
-    for t in range(1, min(3, tiles)):
-        fetch_w(t, t - 1).start()
+    for pair in early:
+        for copy in pair:
+            copy.start()
+    get_x.start()
 
     barrier = pltpu.get_barrier_semaphore()
 
@@ -192,6 +198,19 @@
     grad_share(column(gp_ref[...], me * pieces // n * keep, 8), gs_vm, write)
     signs[1].wait()
     pick_q, hi, lo = hidden_share(me, column(hp_ref[...], 0, sketch), hs_vm, x_hbm.shape)
+    tall = None
+    for j, pair in enumerate(early):
+        for copy in pair:
+            copy.wait()
+        if j == 1 and tiles > 1:
+            fetch_w(1, 0).start()
+        where = slice(j * span, (j + 1) * span)
+        term = dot_nt(w_first[:, where], g_vm[:, where])
+        tall = term if tall is None else tall + term
+    if tiles > 2:
+        fetch_w(2, 1).start()
+    o_vm[0] = tall[:bm].astype(BF)
+    put_out(0).start()
     get_x.wait()
     total = None
     for q in range(blocks):
@@ -200,13 +219,6 @@
         term = dot(both.astype(BF), x_vm[q])
         total = term if total is None else total + term
     part[...] = (total[:sketch] + total[sketch:]) * (length ** -1.5)
-    for copy in get_g:
-        copy.wait()
-    get_w.wait()
-
-    tall = dot_nt(w_first[...], g_vm[...])
-    o_vm[0] = tall[:bm].astype(BF)
-    put_out(0).start()
     own_grad = (tall[bm : bm + 8] + tall[bm + 8 : bm + 16]) * (width ** -1.5)
     rest = send.shape[1] - 2 * keep
     for p in range(pieces):
@@ -255,21 +267,40 @@
     found = recv[0][:keep]
     for j in range(1, n):
         found = found + recv[j][:keep]
-    grads = jnp.concatenate([recv[p * n // pieces][keep : 2 * keep] for p in range(pieces)], axis=0)
+    found_ref[...] = found
+    grads_ref[...] = jnp.concatenate([recv[p * n // pieces][keep : 2 * keep] for p in range(pieces)], axis=0)
+
+    def end_out(t, carry):
+        put_out(t).wait()
+        return carry
+
+    lax.fori_loop(0, tiles, end_out, 0)
+
+
+def last_kernel(found_ref, grads_ref, len_ref, given, out_hbm, sk_ref, held, read_sem, write_sem):
+    parts, rows, tokens = held.shape
+    keep = found_ref.shape[0]
+    seqs = len_ref.shape[1]
+    seq_len = tokens // seqs
+    reads = [pltpu.make_async_copy(given.at[pl.ds(j * rows, rows), :], held.at[j], read_sem.at[j]) for j in range(parts)]
+    writes = [
+        pltpu.make_async_copy(held.at[j], out_hbm.at[pl.ds(j * rows, rows), :], write_sem.at[j]) for j in range(parts)
+    ]
+    for copy in reads:
+        copy.start()
+    for copy, after in zip(reads, writes):
+        copy.wait()
+        after.start()
     lens = column(len_ref[...], 0, seqs)
     places = iota((seqs, tokens), 1)
     live = ((places // seq_len == iota((seqs, tokens), 0)) & (places % seq_len < lens)).astype(F32)
-    left = jnp.concatenate([live * found[a : a + 1] for a in range(keep)], axis=0)
+    left = jnp.concatenate([live * found_ref[a : a + 1, :] for a in range(keep)], axis=0)
     result = lax.dot_general(
-        left, grads, (((1,), (1,)), ((), ())), precision=highest, preferred_element_type=F32
+        left, grads_ref[...], (((1,), (1,)), ((), ())), precision=highest, preferred_element_type=F32
     )
     sk_ref[...] = jnp.concatenate([result[a * seqs : (a + 1) * seqs] for a in range(keep)], axis=1)
-
-    def end_out(t, carry):
-        put_out(t).wait()
-        return carry
-
-    lax.fori_loop(0, tiles, end_out, 0)
+    for copy in writes:
+        copy.wait()
 
 
 def body(hidden_in, out_grad, down_weight, hidden_signs, grad_signs, hidden_picks, grad_picks, seq_lengths):
@@ -289,14 +320,15 @@
     vmem = pl.BlockSpec(memory_space=pltpu.VMEM)
     hbm = pl.BlockSpec(memory_space=pl.ANY)
     dma = pltpu.SemaphoreType.DMA
-    input_grad, example_sketch = pl.pallas_call(
+    input_grad, found, grads = pl.pallas_call(
         functools.partial(kernel, n, keep),
         out_shape=(
             jax.ShapeDtypeStruct((m, tokens), BF),
-            jax.ShapeDtypeStruct((seqs, keep * sketch), F32),
+            jax.ShapeDtypeStruct((keep, tokens), F32),
+            jax.ShapeDtypeStruct((sketch, tokens), F32),
         ),
-        in_specs=[vmem] * 3 + [hbm] * 5,
-        out_specs=(hbm, vmem),
+        in_specs=[vmem] * 2 + [hbm] * 5,
+        out_specs=(hbm, vmem, vmem),
         scratch_shapes=[
             pltpu.VMEM(hidden_signs.shape, jnp.int32),
             pltpu.VMEM(grad_signs.shape, jnp.int32),
@@ -310,7 +342,8 @@
             pltpu.VMEM((n, message, tokens), F32),
             dma((3,)),
             dma((4,)),
-            dma((3,)),
+            dma((4,)),
+            dma((2,)),
             dma((tiles,)),
             dma((n,)),
             dma((n,)),
@@ -324,13 +357,23 @@
     )(
         hidden_picks.reshape(1, sketch),
         grad_picks.reshape(1, sketch),
-        seq_lengths.reshape(1, seqs),
         hidden_signs,
         grad_signs,
         hidden_in,
         out_grad,
         flat_weight,
     )
+    input_grad, example_sketch = pl.pallas_call(
+        last_kernel,
+        out_shape=(
+            jax.ShapeDtypeStruct((m, tokens), BF),
+            jax.ShapeDtypeStruct((seqs, keep * sketch), F32),
+        ),
+        in_specs=[vmem] * 3 + [hbm],
+        out_specs=(hbm, vmem),
+        scratch_shapes=[pltpu.VMEM((tiles, bm, tokens), BF), dma((tiles,)), dma((tiles,))],
+        compiler_params=pltpu.CompilerParams(vmem_limit_bytes=63 * MB),
+    )(found, grads, seq_lengths.reshape(1, seqs), input_grad)
     if share < keep * sketch:
         example_sketch = lax.dynamic_slice_in_dim(example_sketch, rank * share % sketch, share, 1)
     return (input_grad.reshape(blocks, rows, tokens), example_sketch)

time: 30.4 us -> 30 us (0.987)
  local copies, waits for them, and re-layouts: 3.51 us -> 0 us
  Pallas kernels: 26 us -> 29.2 us
    pallas_call x0 -> x1, Pallas kernels: none -> 3.79 us  [body(): pl.pallas_call(last_kernel, out_shape=(jax.ShapeDtypeStruct((m, tokens),...]
    unnamed x4 -> x0, local copies, waits for them, and re-layouts: 3.51 us -> none
    pallas_call x1, Pallas kernels: 26 us -> 25.4 us  [body(): pl.pallas_call(functools.partial(kernel, n, keep), out_shape=(jax.ShapeDt...]
where the time goes in v3:
time: 30 us; the launch traced here: 29.9 us
  Pallas kernels  29.2 us (97%)
  between operations  0.64 us (2%)
    pallas_call x1, Pallas kernels, body(): pl.pallas_call(functools.partial(kernel, n, keep), out_shape=(jax.ShapeDt...  25.4 us
    pallas_call x1, Pallas kernels, body(): pl.pallas_call(last_kernel, out_shape=(jax.ShapeDtypeStruct((m, tokens),...  3.79 us

profile of v3, /device:TPU:8, one launch (start us, length us, event | category | flops | bytes accessed | tf_op | source)
XLA Modules:
  0.0 29.9 jit_solution(5110014295795701797)
XLA Ops:
  0.6 25.4 %shard_map.95 = (bf16[1792,512]{1,0:T(8,128)(2,1)}, f32[4,512]{1,0:T(4,128)}, f32[64,512]{1,0:T(8,128)}) custom-call(s32[1,64]{1,0:T(1,128)} %bitcast.8, s32[1,64]{1,0:T(1,128)} %bitcast.9, s32[3,7,4096]{2,1,0:T(8,128)} %hs_hbm.1, s32[3,8192]{1,0:T(4,128)} %gs_hbm.1, bf16[7,256,512]{2,1,0:T(8,128)(2,1)} %x_hbm.1, bf16[512,8192]{1,0:T(8,128)(2,1)} %g_hbm.1, ...), custom_call_target="tpu_custom_call" | custom-call | flops 15032385536 | bytes 37748736 | tf_op jit(solution)/shard_map/pallas_call | solution.py:323
  26.1 3.8 %shard_map.96 = (bf16[1792,512]{1,0:T(8,128)(2,1)}, f32[8,256]{1,0:T(8,128)}) custom-call(f32[4,512]{1,0:T(4,128)} %get-tuple-element.7.found_ref, f32[64,512]{1,0:T(8,128)} %get-tuple-element.8.grads_ref, s32[1,8]{1,0:T(1,128)} %bitcast.5, bf16[1792,512]{1,0:T(8,128)(2,1)} %get-tuple-element.9.given), custom_call_target="tpu_custom_call" | custom-call | tf_op jit(solution)/shard_map/pallas_call | solution.py:366

commit v4 on v3

--- a/solution.py
+++ b/solution.py
@@ -277,7 +277,9 @@
     lax.fori_loop(0, tiles, end_out, 0)
 
 
-def last_kernel(found_ref, grads_ref, len_ref, given, out_hbm, sk_ref, held, read_sem, write_sem):
+def last_kernel(
+    found_hbm, grads_hbm, len_hbm, given, out_hbm, sk_hbm, found_ref, grads_ref, len_ref, sk_ref, held, small_sem, read_sem, write_sem
+):
     parts, rows, tokens = held.shape
     keep = found_ref.shape[0]
     seqs = len_ref.shape[1]
@@ -286,8 +288,16 @@
     writes = [
         pltpu.make_async_copy(held.at[j], out_hbm.at[pl.ds(j * rows, rows), :], write_sem.at[j]) for j in range(parts)
     ]
-    for copy in reads:
+    small = [
+        pltpu.make_async_copy(found_hbm, found_ref, small_sem.at[0]),
+        pltpu.make_async_copy(grads_hbm, grads_ref, small_sem.at[1]),
+        pltpu.make_async_copy(len_hbm, len_ref, small_sem.at[2]),
+    ]
+    put_sketch = pltpu.make_async_copy(sk_ref, sk_hbm, small_sem.at[3])
+    for copy in small + reads:
         copy.start()
+    for copy in small:
+        copy.wait()
     for copy, after in zip(reads, writes):
         copy.wait()
         after.start()
@@ -299,8 +309,10 @@
         left, grads_ref[...], (((1,), (1,)), ((), ())), precision=highest, preferred_element_type=F32
     )
     sk_ref[...] = jnp.concatenate([result[a * seqs : (a + 1) * seqs] for a in range(keep)], axis=1)
+    put_sketch.start()
     for copy in writes:
         copy.wait()
+    put_sketch.wait()
 
 
 def body(hidden_in, out_grad, down_weight, hidden_signs, grad_signs, hidden_picks, grad_picks, seq_lengths):
@@ -369,9 +381,18 @@
             jax.ShapeDtypeStruct((m, tokens), BF),
             jax.ShapeDtypeStruct((seqs, keep * sketch), F32),
         ),
-        in_specs=[vmem] * 3 + [hbm],
-        out_specs=(hbm, vmem),
-        scratch_shapes=[pltpu.VMEM((tiles, bm, tokens), BF), dma((tiles,)), dma((tiles,))],
+        in_specs=[hbm] * 4,
+        out_specs=(hbm, hbm),
+        scratch_shapes=[
+            pltpu.VMEM((keep, tokens), F32),
+            pltpu.VMEM((sketch, tokens), F32),
+            pltpu.VMEM((1, seqs), jnp.int32),
+            pltpu.VMEM((seqs, keep * sketch), F32),
+            pltpu.VMEM((tiles, bm, tokens), BF),
+            dma((4,)),
+            dma((tiles,)),
+            dma((tiles,)),
+        ],
         compiler_params=pltpu.CompilerParams(vmem_limit_bytes=63 * MB),
     )(found, grads, seq_lengths.reshape(1, seqs), input_grad)
     if share < keep * sketch:

time: 30 us -> 28.9 us (0.963)
  Pallas kernels: 29.2 us -> 28.1 us
    pallas_call x1, Pallas kernels: 3.79 us -> 2.7 us  [body(): pl.pallas_call(last_kernel, out_shape=(jax.ShapeDtypeStruct((m, tokens),...]
where the time goes in v4:
time: 28.9 us; the launch traced here: 28.8 us
  Pallas kernels  28.1 us (97%)
  between operations  0.64 us (2%)
    pallas_call x1, Pallas kernels, body(): pl.pallas_call(functools.partial(kernel, n, keep), out_shape=(jax.ShapeDt...  25.4 us
    pallas_call x1, Pallas kernels, body(): pl.pallas_call(last_kernel, out_shape=(jax.ShapeDtypeStruct((m, tokens),...  2.7 us

profile of v4, /device:TPU:8, one launch (start us, length us, event | category | flops | bytes accessed | tf_op | source)
XLA Modules:
  0.0 28.8 jit_solution(13119367123445546746)
XLA Ops:
  0.6 25.4 %shard_map.95 = (bf16[1792,512]{1,0:T(8,128)(2,1)}, f32[4,512]{1,0:T(4,128)}, f32[64,512]{1,0:T(8,128)}) custom-call(s32[1,64]{1,0:T(1,128)} %bitcast.8, s32[1,64]{1,0:T(1,128)} %bitcast.9, s32[3,7,4096]{2,1,0:T(8,128)} %hs_hbm.1, s32[3,8192]{1,0:T(4,128)} %gs_hbm.1, bf16[7,256,512]{2,1,0:T(8,128)(2,1)} %x_hbm.1, bf16[512,8192]{1,0:T(8,128)(2,1)} %g_hbm.1, ...), custom_call_target="tpu_custom_call" | custom-call | flops 15032385536 | bytes 37748736 | tf_op jit(solution)/shard_map/pallas_call | solution.py:335
  26.1 2.7 %shard_map.96 = (bf16[1792,512]{1,0:T(8,128)(2,1)}, f32[8,256]{1,0:T(8,128)}) custom-call(f32[4,512]{1,0:T(4,128)} %get-tuple-element.7.found_hbm, f32[64,512]{1,0:T(8,128)} %get-tuple-element.8.grads_hbm, s32[1,8]{1,0:T(1,128)} %bitcast.5, bf16[1792,512]{1,0:T(8,128)(2,1)} %get-tuple-element.9.given), custom_call_target="tpu_custom_call" | custom-call | tf_op jit(solution)/shard_map/pallas_call | solution.py:378
